TPU v7x, 32 devices: a whole 2x2x4 slice. The times are simulated.
32 devices in a mesh: rows: 8 (over z, core), cols: 4 (over y, x).
Axes of the slice: x: 2, y: 2, z: 4, core: 2. Of those that a mesh axis runs over, the one named last changes fastest.
Arguments:
- slm_field: float32 [2, 2048, 1024], P(None, 'rows', 'cols'), may hold values from -6 to 6
- target_light: float32 [16, 8, 256], P('rows', 'cols'), may hold values from 0 to 0.5
Outputs:
- gradient: float32 [2, 2048, 1024], P(None, 'rows', 'cols')
- light_field: float32 [16, 8, 256], P('rows', 'cols')
All inputs are finite; a program needn't handle non-finite values.
Results may differ from a plain program's by a relative error of at most 0.012.
Values may be sent and summed in bfloat16 or wider, within the bound.
No kernel may reach another device: no remote copies, remote signals or barrier semaphores. Data moves between devices by JAX's collectives and lax.ppermute only.
A program may use at most 64 MiB of HBM per device.

v0:
```python
import math

import jax
import jax.numpy as jnp
import ml_dtypes
import numpy as np
from jax import lax
from jax.experimental import pallas as pl
from jax.experimental.pallas import tpu as pltpu
from jax.sharding import PartitionSpec as P

WIN = 256
VIEWS = 16
STRIDE = 128
BIN = 16

distance_px = 16000.0
index_ratio = 15.0

BF16 = jnp.bfloat16
F32 = jnp.float32
BOTH_MINOR = (((1,), (1,)), ((), ()))


def call(body, outs, args, scratch=(), flops=0, in_specs=None, out_specs=None):
    nbytes = sum(math.prod(a.shape) * a.dtype.itemsize for a in (*outs, *args))
    specs = {}
    if in_specs:
        whole = pl.BlockSpec(memory_space=pltpu.VMEM)
        specs["in_specs"] = [in_specs.get(n, whole) for n in range(len(args))]
    if out_specs:
        specs["out_specs"] = out_specs
    return pl.pallas_call(
        body,
        out_shape=outs,
        scratch_shapes=list(scratch),
        compiler_params=pltpu.CompilerParams(vmem_limit_bytes=24 * 2**20),
        cost_estimate=pl.CostEstimate(flops=flops, bytes_accessed=nbytes, transcendentals=0),
        **specs,
    )(*args)


def shape_of(dims, dtype):
    return jax.ShapeDtypeStruct(dims, dtype)


def high_low(table):
    table = np.asarray(table, np.float32)
    high = table.astype(ml_dtypes.bfloat16)
    low = (table - high.astype(np.float32)).astype(ml_dtypes.bfloat16)
    return np.concatenate([high, low], axis=0)


def times_i(values):
    half = values.shape[-1] // 2
    if values.shape[-1] == 128:
        lanes = lax.broadcasted_iota(jnp.int32, values.shape, values.ndim - 1)
        turned = pltpu.roll(values, half, values.ndim - 1)
        return jnp.where(lanes < half, -turned, turned)
    return jnp.concatenate([-values[..., half:], values[..., :half]], axis=-1)


def rounded_with_i(value):
    rounded = value.astype(BF16)
    half = value.shape[-1] // 2
    if half % 128:
        return rounded, times_i(value.astype(F32)).astype(BF16)
    return rounded, jnp.concatenate([-rounded[:, half:], rounded[:, :half]], axis=1)


def small_dft(points, sign):
    count = len(points)
    if count == 1:
        return points
    even = small_dft(points[0::2], sign)
    odd = small_dft(points[1::2], sign)
    front, back = [], []
    for k in range(count // 2):
        re, im = odd[k]
        angle = sign * 2.0 * math.pi * k / count
        cosine, sine = math.cos(angle), math.sin(angle)
        if k == 0:
            pass
        elif 4 * k == count:
            re, im = (-im, re) if sign > 0 else (im, -re)
        elif 8 * k == count:
            re, im = cosine * (re - sign * im), cosine * (im + sign * re)
        elif 8 * k == 3 * count:
            re, im = cosine * (re + sign * im), cosine * (im - sign * re)
        else:
            re, im = re * cosine - im * sine, re * sine + im * cosine
        even_re, even_im = even[k]
        front.append((even_re + re, even_im + im))
        back.append((even_re - re, even_im - im))
    return front + back


def packed_dft(points, sign):
    count = len(points)
    if count == 1:
        return points
    even = packed_dft(points[0::2], sign)
    odd = packed_dft(points[1::2], sign)
    front, back = [], []
    for k in range(count // 2):
        term = odd[k]
        angle = sign * 2.0 * math.pi * k / count
        if 4 * k == count:
            term = times_i(term) if sign > 0 else -times_i(term)
        elif k:
            term = math.cos(angle) * term + math.sin(angle) * times_i(term)
        front.append(even[k] + term)
        back.append(even[k] - term)
    return front + back


def turn(rows, cols, period, sign):
    angles = sign * 2.0 * np.pi / period * ((np.arange(rows)[:, None] * np.arange(cols)) % period)
    return np.cos(angles), np.sin(angles)


def block_diagonal(block, copies):
    return np.kron(np.eye(copies), block)


class Plan:
    def __init__(self, rows_count, cols_count, rows_dev, cols_dev):
        self.R, self.C = rows_count, cols_count
        self.D = rows_count * cols_count
        self.X = cols_dev
        self.m = rows_dev // cols_count
        self.lanes = 2 * self.m
        self.P = 128 // self.m
        self.span = cols_dev // rows_count
        self.f = self.span // self.P
        self.total_rows = rows_dev * rows_count
        self.total_cols = cols_dev * cols_count
        self.outer = 8
        self.inner = self.D // 8
        self.shift = STRIDE // self.m
        self.hogel_rows = self.total_rows // STRIDE
        self.hogel_cols = self.total_cols // STRIDE
        self.parts = self.D // self.hogel_rows
        self.pp = WIN // self.parts
        self.views = VIEWS // self.parts
        self.own_cols = cols_dev // STRIDE

    def place(self, s):
        return s % self.C * self.R + s // self.C

    def line_tables(self, sign):
        cosine, sine = turn(self.X, self.X, self.X, sign)
        weights = high_low(np.concatenate([cosine, sine], axis=1)).reshape(2, self.X, 2 * self.X)
        twist = turn(self.X, self.C, self.total_cols, sign)
        return weights, np.concatenate(twist, axis=1).astype(np.float32)

    def pencil_tables(self):
        cosine, sine = turn(self.m, self.m, self.m, -1.0)
        cosine, sine = block_diagonal(cosine, self.P), block_diagonal(sine, self.P)
        ahead = np.block([[cosine, sine], [-sine, cosine]])
        behind = np.block([[cosine, -sine], [sine, cosine]]) / (self.total_rows * self.total_cols)
        twist = turn(self.D, self.m, self.total_rows, -1.0)
        twist = np.stack([np.tile(part, (1, self.P)) for part in twist]).astype(np.float32)
        return high_low(ahead), high_low(behind), twist

    def row_table(self, real, imag):
        blocks = []
        for slab in range(WIN // self.m):
            rows = slice(slab * self.m, (slab + 1) * self.m)
            for left, right in ((real[rows], imag[rows]), (-imag[rows], real[rows])):
                pieces = []
                for part in range(self.parts):
                    cols = slice(part * self.pp, (part + 1) * self.pp)
                    pieces += [left[:, cols], right[:, cols]]
                blocks.append(np.concatenate(pieces, axis=1))
        return np.concatenate(blocks, axis=0)

    def group_table(self):
        return np.kron(np.eye(self.views), np.ones((BIN, BIN))).astype(np.float32)


def hogel_tables():
    positions = np.arange(WIN)
    tapers = np.sin(np.pi * (positions + 0.5) / WIN) ** 2
    angles = -2.0 * np.pi / WIN * (positions[:, None] * positions[None, :] % WIN)
    cosine = (tapers[:, None] * np.cos(angles)).astype(np.float32)
    sine = (tapers[:, None] * np.sin(angles)).astype(np.float32)
    col = np.concatenate([cosine, sine], axis=1).astype(ml_dtypes.bfloat16)
    col_turned = np.concatenate([cosine.T, sine.T], axis=1).astype(ml_dtypes.bfloat16)
    row = np.stack([cosine / WIN, sine / WIN]).astype(ml_dtypes.bfloat16)
    return col, col_turned, row


def three_pieces(values):
    first = values.astype(BF16)
    rest = values - first.astype(F32)
    second = rest.astype(BF16)
    return first, second, (rest - second.astype(F32)).astype(BF16)


def matmul(left, right):
    return jnp.dot(left, right, preferred_element_type=F32)


def partners(count):
    return sorted(range(count), key=lambda t: (t != 0, -t.bit_count()))


def gather_chunks(arrived, chunks):
    mine = lax.axis_index("cols")
    for t, chunk in zip(partners(len(arrived)), arrived):
        chunks[mine ^ t] = chunk[...]


def scatter_chunks(chunks, leaving):
    mine = lax.axis_index("cols")
    for t, chunk in zip(partners(len(leaving)), leaving):
        chunk[...] = chunks[mine ^ t]


def put_views(plan, rows):
    pad = jnp.zeros((VIEWS - 3 * plan.own_cols, plan.lanes), F32)
    pieces = [piece.astype(F32) for piece in three_pieces(rows)]
    return jnp.concatenate([*pieces, pad], axis=0).astype(BF16)


def get_views(plan, chunk):
    chunk = chunk.astype(F32)
    n = plan.own_cols
    return chunk[:n] + chunk[n : 2 * n] + chunk[2 * n : 3 * n]


def pack_kernel(plan, field, goal, *refs):
    C, m, X = plan.C, plan.m, plan.X
    leaving, (out,) = refs[:C], refs[C:]
    for c in range(C):
        rows = slice(c * m, (c + 1) * m)
        block = jnp.concatenate([field[0, rows, :], field[1, rows, :]], axis=0)
        out[c, :X, :] = block.astype(F32).T.astype(BF16)
        i, start = c // plan.parts, c % plan.parts * plan.lanes
        out[c, X:, :] = put_views(plan, goal[i, :, start : start + plan.lanes])
    scatter_chunks(out, leaving)


def unpack_kernel(plan, *refs):
    C, m, X = plan.C, plan.m, plan.X
    arrived, (out, light, slabs) = refs[:C], refs[C:]
    gather_chunks(arrived, slabs)
    for c in range(C):
        block = slabs[c, :X, :].astype(F32).T
        out[0, m * c : m * c + m, :] = block[:m]
        out[1, m * c : m * c + m, :] = block[m:]
        i, start = c // plan.parts, c % plan.parts * plan.lanes
        light[i, :, start : start + plan.lanes] = get_views(plan, slabs[c, X:, :])


def lines_forward(plan, lanes, load, emit, weights, twist, turned):
    C, X = plan.C, plan.X
    step = 64
    for start in range(0, X, step):
        points = packed_dft([load(c, start, step) for c in range(C)], -1.0)
        for k in range(C):
            cosine = twist[start : start + step, k : k + 1]
            sine = twist[start : start + step, C + k : C + k + 1]
            value = points[k]
            if lanes % 256:
                across = times_i(value)
                if k:
                    value, across = value * cosine + across * sine, across * cosine - value * sine
                value, across = value.astype(BF16), across.astype(BF16)
            else:
                if k:
                    value = value * cosine + times_i(value) * sine
                value, across = rounded_with_i(value)
            place = slice(k * lanes, k * lanes + lanes)
            turned[start : start + step, place] = value
            turned[X + start : X + start + step, place] = across
    group = max(1, 256 // lanes)
    for first in range(0, C, group):
        result = matmul(weights[...], turned[:, first * lanes : (first + group) * lanes])
        for k in range(group):
            for r in range(plan.R):
                rows = slice(r * plan.span, (r + 1) * plan.span)
                emit((first + k) * plan.R + r, result[rows, k * lanes : (k + 1) * lanes])


def lines_inverse(plan, lanes, product, emit, twist):
    C, X = plan.C, plan.X
    step = 64
    for start in range(0, X, step):
        rows = slice(start, start + step)
        result = product(rows)
        points = []
        for k in range(C):
            value = result[:, k * lanes : (k + 1) * lanes]
            if k:
                cosine, sine = twist[rows, k : k + 1], twist[rows, C + k : C + k + 1]
                value = value * cosine + times_i(value) * sine
            points.append(value)
        for c, value in enumerate(packed_dft(points, 1.0)):
            emit(c, start, step, value)


def to_planes(plan, block):
    parts = [block[p * plan.f : (p + 1) * plan.f, :] for p in range(plan.P)]
    real = jnp.concatenate([part[:, : plan.m] for part in parts], axis=1)
    imag = jnp.concatenate([part[:, plan.m :] for part in parts], axis=1)
    return real, imag


def from_planes(plan, real, imag):
    m = plan.m
    return jnp.concatenate(
        [
            jnp.concatenate([real[:, p * m : (p + 1) * m], imag[:, p * m : (p + 1) * m]], axis=1)
            for p in range(plan.P)
        ],
        axis=0,
    )


def rows_forward_kernel(plan, weights, twist, *refs):
    C, X = plan.C, plan.X
    arrived, (_, _, out, goals, turned, slabs) = refs[:C], refs[C:]
    gather_chunks(arrived, slabs)
    goals[...] = slabs[:, X:, :]

    def load(c, start, step):
        return slabs[c, start : start + step, :].astype(F32)

    def emit(d, block):
        out[d] = jnp.concatenate(to_planes(plan, block), axis=0).astype(BF16)

    lines_forward(plan, plan.lanes, load, emit, weights, twist, turned)


def rows_inverse_kernel(plan, pencils, lights, weights, twist, *refs):
    C, X, lanes = plan.C, plan.X, plan.lanes
    leaving, (packed, out) = refs[:C], refs[C:]
    for k in range(C):
        for r in range(plan.R):
            chunk = pencils[k * plan.R + r].astype(F32)
            block = from_planes(plan, chunk[: plan.f], chunk[plan.f :])
            place = slice(k * lanes, k * lanes + lanes)
            packed[r * plan.span : (r + 1) * plan.span, place] = block.astype(BF16)
            packed[X + r * plan.span : X + (r + 1) * plan.span, place] = times_i(block).astype(BF16)

    def emit(c, start, step, value):
        out[c, start : start + step, :] = value.astype(BF16)

    def product(rows):
        return matmul(weights[0, rows, :], packed[...]) + matmul(weights[1, rows, :], packed[...])

    lines_inverse(plan, lanes, product, emit, twist)
    out[:, X:, :] = lights[...]
    scatter_chunks(out, leaving)


def columns(plan, sign, load, store, steer_re, steer_im, ahead, behind, twist, scratch):
    D, f, outer, inner = plan.D, plan.f, plan.outer, plan.inner
    half_re, half_im, rounded = scratch
    for b in range(inner):
        points = [load(inner * a + b) for a in range(outer)]
        for alpha, (re, im) in enumerate(small_dft(points, -1.0)):
            angle = -2.0 * math.pi * b * alpha / D
            cosine, sine = math.cos(angle), math.sin(angle)
            if b * alpha:
                re, im = re * cosine - im * sine, re * sine + im * cosine
            half_re[alpha * inner + b] = re
            half_im[alpha * inner + b] = im
    for alpha in range(outer):
        points = [(half_re[alpha * inner + b], half_im[alpha * inner + b]) for b in range(inner)]
        for beta, (re, im) in enumerate(small_dft(points, -1.0)):
            k = alpha + outer * beta
            cosine, sine = twist[0, k : k + 1, :], twist[1, k : k + 1, :]
            for offset, part in ((0, re * cosine - im * sine), (128, re * sine + im * cosine)):
                rounded[k, :, offset : offset + 128] = part.astype(BF16)
    group = D // 8 if sign > 0 else D
    for start in range(0, D, group):
        place = slice(start, start + group)

        def multiply(matrix):
            left = rounded[place].reshape(group * f, 256)
            product = matmul(left, matrix[:256, :]) + matmul(left, matrix[256:, :])
            return product.reshape(group, f, 256)

        result = multiply(ahead)
        re, im = result[:, :, :128], result[:, :, 128:]
        factor_re, factor_im = steer_re[place], sign * steer_im[place]
        for offset, part in (
            (0, re * factor_re - im * factor_im),
            (128, re * factor_im + im * factor_re),
        ):
            rounded[place, :, offset : offset + 128] = part.astype(BF16)
        result = multiply(behind)
        half_re[place] = result[:, :, :128]
        half_im[place] = result[:, :, 128:]
    for alpha in range(outer):
        points = []
        for beta in range(inner):
            k = alpha + outer * beta
            cosine, sine = twist[0, k : k + 1, :], twist[1, k : k + 1, :]
            re, im = half_re[k], half_im[k]
            points.append((re * cosine + im * sine, im * cosine - re * sine))
        for b, (re, im) in enumerate(small_dft(points, 1.0)):
            angle = 2.0 * math.pi * b * alpha / D
            cosine, sine = math.cos(angle), math.sin(angle)
            if b * alpha:
                re, im = re * cosine - im * sine, re * sine + im * cosine
            half_re[alpha + outer * b] = re
            half_im[alpha + outer * b] = im
    for b in range(inner):
        points = [(half_re[alpha + outer * b], half_im[alpha + outer * b]) for alpha in range(outer)]
        for a, (re, im) in enumerate(small_dft(points, 1.0)):
            store(inner * a + b, re, im)


def pencil_forward_kernel(plan, pencils, *refs):
    steer_re, steer_im, ahead, behind, twist, row, out, windows, *scratch = refs
    f, lanes, span = plan.f, plan.lanes, plan.span

    def load(s):
        chunk = pencils[plan.place(s)].astype(F32)
        return chunk[:f], chunk[f:]

    def store(s, re, im):
        block = from_planes(plan, re, im).astype(BF16)
        i, slab = s // plan.shift, s % plan.shift
        windows[i, :, slab * lanes : (slab + 1) * lanes] = block
        slab += plan.shift
        windows[(i - 1) % plan.hogel_rows, :, slab * lanes : (slab + 1) * lanes] = block

    columns(plan, 1.0, load, store, steer_re, steer_im, ahead, behind, twist, scratch)
    count = plan.hogel_rows
    result = matmul(windows[...].reshape(count * span, 2 * WIN), row[...]).astype(BF16)
    for i in range(count):
        for part in range(plan.parts):
            out[plan.place(i * plan.parts + part)] = result[
                i * span : (i + 1) * span, part * 2 * plan.pp : (part + 1) * 2 * plan.pp
            ]


def pencil_back_kernel(plan, lines, *refs):
    steer_re, steer_im, ahead, behind, twist, row, out, windows, *scratch = refs
    lanes, span, parts = plan.lanes, plan.span, plan.parts
    count, wide = plan.hogel_rows, 2 * plan.pp
    result = 0.0
    for n in range(parts):
        own = jnp.stack([lines[plan.place(i * parts + n)] for i in range(count)])
        before = jnp.concatenate([own[-1:], own[:-1]], axis=0)
        depth = slice(n * wide, (n + 1) * wide)
        result = result + matmul(own.reshape(count * span, wide), row[depth, :WIN])
        result = result + matmul(before.reshape(count * span, wide), row[depth, WIN:])
    windows[...] = result.reshape(count, span, WIN)

    def load(s):
        i, slab = s // plan.shift, s % plan.shift
        return to_planes(plan, windows[i, :, slab * lanes : (slab + 1) * lanes])

    def store(s, re, im):
        out[plan.place(s)] = jnp.concatenate([re, im], axis=0).astype(BF16)

    columns(plan, -1.0, load, store, steer_re, steer_im, ahead, behind, twist, scratch)


def hogel_kernel(plan, lines, goals, *refs):
    weights_behind, twist_behind, weights_ahead, twist_ahead, col, col_turned, same = refs[:7]
    out, lights, packed, field, spectra, bright, factors, weighted, back = refs[7:]
    C, X, lanes, pp = plan.C, plan.X, 2 * plan.pp, plan.pp
    total = plan.total_cols
    for k in range(C):
        block = lines[k * plan.R : (k + 1) * plan.R].reshape(X, lanes)
        place = slice(k * lanes, (k + 1) * lanes)
        packed[:X, place], packed[X:, place] = rounded_with_i(block)

    def emit_near(c, start, step, value):
        for n, rounded in enumerate(rounded_with_i(value)):
            field[n, c * X + start : c * X + start + step, :] = rounded
            if c == 0 and start < STRIDE:
                field[n, total + start : total + start + step, :] = rounded

    near = matmul(weights_behind[0], packed[...])
    lines_inverse(plan, lanes, lambda rows: near[rows, :], emit_near, twist_behind)
    for j in range(plan.hogel_cols):
        window = slice(STRIDE * j, STRIDE * j + WIN)
        result = matmul(
            col_turned[...], jnp.concatenate([field[0, window, :], field[1, window, :]], axis=0)
        )
        spectra[j] = result
        power = result[:, :pp] * result[:, :pp] + result[:, pp:] * result[:, pp:]
        bright[j * VIEWS : (j + 1) * VIEWS, :] = power.reshape(VIEWS, BIN, pp).sum(axis=1)
    exact = lax.Precision.HIGHEST
    own = lax.broadcasted_iota(jnp.int32, (VIEWS, pp), 0) == (
        lax.broadcasted_iota(jnp.int32, (VIEWS, pp), 1) % VIEWS
    )
    for c in range(C):
        target = get_views(plan, goals[c])
        for j in range(plan.own_cols):
            h = c * plan.own_cols + j
            below = (plan.hogel_cols + h) * VIEWS
            bright[below : below + VIEWS, :] = jnp.where(own, target[j : j + 1, :], 0.0)
    spread = jnp.dot(bright[...], same[...], preferred_element_type=F32, precision=exact)
    views = plan.hogel_cols * VIEWS
    light = spread[:views] * (1.0 / (BIN * BIN))
    factors[...] = 4.0 * (light - spread[views:])
    bright[:views, :] = light
    for c in range(C):
        rows = []
        for j in range(plan.own_cols):
            h = c * plan.own_cols + j
            block = jnp.where(own, bright[h * VIEWS : (h + 1) * VIEWS, :], 0.0)
            rows.append(jnp.sum(block, axis=0, keepdims=True))
        lights[c] = put_views(plan, jnp.concatenate(rows, axis=0))
    for j in range(plan.hogel_cols):
        for view in range(VIEWS):
            factor = factors[j * VIEWS + view : j * VIEWS + view + 1, :]
            block = slice(view * BIN, (view + 1) * BIN)
            below = slice(WIN + view * BIN, WIN + (view + 1) * BIN)
            real = (spectra[j, block, :pp] * factor).astype(BF16)
            imag = (spectra[j, block, pp:] * factor).astype(BF16)
            weighted[block, :pp] = real
            weighted[block, pp:] = imag
            weighted[below, :pp] = imag
            weighted[below, pp:] = -real
        result = matmul(col[...], weighted[...])
        first = slice(STRIDE * j, STRIDE * (j + 1))
        back[first] = result[:STRIDE] if j == 0 else pending + result[:STRIDE]
        pending = result[STRIDE:]
    back[:STRIDE] = back[:STRIDE] + pending

    def load(c, start, step):
        return back[c * X + start : c * X + start + step, :]

    def emit(d, block):
        out[d] = block.astype(BF16)

    lines_forward(plan, lanes, load, emit, weights_ahead, twist_ahead, packed)


def steer_table(plan):
    index = lax.axis_index(("cols", "rows"))
    shape = (plan.D, plan.f, 128)
    k = lax.broadcasted_iota(jnp.int32, shape, 0)
    line = lax.broadcasted_iota(jnp.int32, shape, 1)
    lane = lax.broadcasted_iota(jnp.int32, shape, 2)
    u = k + plan.D * (lane % plan.m)
    v = index // plan.R + plan.C * (
        plan.span * (index % plan.R) + plan.f * (lane // plan.m) + line
    )

    def freq(position, count):
        return ((position + count // 2) % count - count // 2).astype(F32) / count

    freq_rows, freq_cols = freq(u, plan.total_rows), freq(v, plan.total_cols)
    radial = freq_rows * freq_rows + freq_cols * freq_cols
    phase = (
        -2.0
        * math.pi
        * distance_px
        * radial
        / (jnp.sqrt(index_ratio * index_ratio - radial) + index_ratio)
    )
    return jnp.cos(phase), jnp.sin(phase)


def exchange(chunks):
    return lax.all_to_all(chunks, ("cols", "rows"), split_axis=0, concat_axis=0, tiled=True)


def swap_columns(chunks):
    count = lax.axis_size("cols")
    return tuple(
        lax.ppermute(chunk, "cols", [(i, i ^ t) for i in range(count)]) if t else chunk
        for t, chunk in zip(partners(count), chunks)
    )


def local(slm_field, target_light):
    rows_count, cols_count = lax.axis_size("rows"), lax.axis_size("cols")
    plan = Plan(rows_count, cols_count, slm_field.shape[1], slm_field.shape[2])
    C, D, X, lanes, f = plan.C, plan.D, plan.X, plan.lanes, plan.f
    span, wide = plan.span, 2 * plan.pp

    ahead, behind, twist = (jnp.asarray(t) for t in plan.pencil_tables())
    weights_ahead, twist_ahead = plan.line_tables(-1.0)
    weights_ahead, twist_ahead = jnp.asarray(weights_ahead[0]), jnp.asarray(twist_ahead)
    weights_behind, twist_behind = (jnp.asarray(t) for t in plan.line_tables(1.0))
    col, col_turned, row = hogel_tables()
    row = plan.row_table(row[0], row[1])
    col, col_turned, row, row_turned, same = (
        jnp.asarray(t) for t in (col, col_turned, row, row.T.copy(), plan.group_table())
    )
    steer_re, steer_im = steer_table(plan)

    slabs_shapes = (shape_of((X + VIEWS, lanes), BF16),) * C
    slabs_scratch = pltpu.VMEM((C, X + VIEWS, lanes), BF16)
    views_shape = shape_of((C, VIEWS, lanes), BF16)
    pencil_shape = shape_of((D, 2 * f, 128), BF16)
    lines_shape = shape_of((D, span, wide), BF16)
    columns_scratch = (
        pltpu.VMEM((D, f, 128), F32),
        pltpu.VMEM((D, f, 128), F32),
        pltpu.VMEM((D, f, 256), BF16),
    )
    pencil_tables = (steer_re, steer_im, ahead, behind, twist)
    columns_flops = 8 * D * f * 256 * 256 + 2 * plan.hogel_rows * span * (2 * WIN) ** 2

    apart_any = pl.BlockSpec(memory_space=pl.ANY)
    slabs = call(
        lambda *refs: pack_kernel(plan, *refs),
        slabs_shapes,
        (slm_field.astype(BF16), target_light),
        (slabs_scratch,),
    )
    tall = pltpu.VMEM((2 * X, C * lanes), BF16)
    pencils, goals = call(
        lambda *refs: rows_forward_kernel(plan, *refs),
        (pencil_shape, views_shape),
        (weights_ahead, twist_ahead, *swap_columns(slabs), steer_re, steer_im),
        (tall, slabs_scratch),
        flops=2 * X * 2 * X * C * lanes,
        in_specs={C + 2: apart_any, C + 3: apart_any},
    )
    (lines,) = call(
        lambda *refs: pencil_forward_kernel(plan, *refs),
        (lines_shape,),
        (exchange(pencils), *pencil_tables, row),
        (pltpu.VMEM((plan.hogel_rows, span, 2 * WIN), BF16), *columns_scratch),
        flops=columns_flops,
    )
    tall = pltpu.VMEM((2 * X, C * wide), BF16)
    lines, lights = call(
        lambda *refs: hogel_kernel(plan, *refs),
        (lines_shape, views_shape),
        (
            exchange(lines),
            goals,
            weights_behind,
            twist_behind,
            weights_ahead,
            twist_ahead,
            col,
            col_turned,
            same,
        ),
        (
            tall,
            pltpu.VMEM((2, plan.total_cols + STRIDE, wide), BF16),
            pltpu.VMEM((plan.hogel_cols, WIN, wide), F32),
            pltpu.VMEM((2 * plan.hogel_cols * VIEWS, plan.pp), F32),
            pltpu.VMEM((plan.hogel_cols * VIEWS, plan.pp), F32),
            pltpu.VMEM((2 * WIN, wide), BF16),
            pltpu.VMEM((plan.total_cols, wide), F32),
        ),
        flops=4 * X * 2 * X * C * wide + 4 * plan.hogel_cols * WIN * 2 * WIN * wide,
    )
    (pencils,) = call(
        lambda *refs: pencil_back_kernel(plan, *refs),
        (pencil_shape,),
        (exchange(lines), *pencil_tables, row_turned),
        (pltpu.VMEM((plan.hogel_rows, span, WIN), F32), *columns_scratch),
        flops=columns_flops,
    )
    tall = pltpu.VMEM((2 * X, C * lanes), BF16)
    slabs = call(
        lambda *refs: rows_inverse_kernel(plan, *refs),
        slabs_shapes,
        (exchange(pencils), lights, weights_behind, twist_behind),
        (tall, slabs_scratch),
        flops=2 * X * 2 * X * C * lanes,
    )
    return call(
        lambda *refs: unpack_kernel(plan, *refs),
        (shape_of(slm_field.shape, F32), shape_of(target_light.shape, F32)),
        swap_columns(slabs),
        (slabs_scratch,),
    )


def solution(mesh):
    return jax.shard_map(
        local,
        mesh=mesh,
        in_specs=(P(None, "rows", "cols"), P("rows", "cols", None)),
        out_specs=(P(None, "rows", "cols"), P("rows", "cols", None)),
        check_vma=False,
    )
```

profile of v0, /device:TPU:0, one launch (start us, length us, event | category | flops | bytes accessed | tf_op | source)
XLA Modules:
  0.0 92.7 jit_solution(7633057667329415541)
XLA Ops:
  0.6 0.0 copy-start.9
  0.6 1.1 %convert_element_type.9.refs_0_ = bf16[2,256,256]{2,1,0:T(8,128)(2,1)S(1)} convert(f32[2,256,256]{2,1,0:T(8,128)} %param.14) | non-fusion elementwise | flops 131072 | bytes 786432 | tf_op jit(solution)/shard_map/convert_element_type | solution.py:612
  1.7 0.0 copy-done.9
  1.7 0.2 shard_map.149
  1.9 4.0 %collective-permute-start = (bf16[272,128]{1,0:T(8,128)(2,1)S(1)}, bf16[272,128]{1,0:T(8,128)(2,1)S(1)}, u32[]{:S(2)}, u32[]{:S(2)}) collective-permute-start(bf16[272,128]{1,0:T(8,128)(2,1)S(1)} %get-tuple-element.15), channel_id=1, source_target_pairs={{0,3},{1,2},{2,1},{3,0},{4,7},{5,6},{6,5},{7,4},{8,11},{9,10},{10,... | collective-permute-start | bytes 208904 | tf_op jit(solution)/shard_map/ppermute | solution.py:573
  5.9 0.5 collective-permute-start.1
  6.4 0.1 collective-permute-start.2
  6.5 0.0 copy-start.5
  6.6 0.0 copy-start.8
  6.6 1.1 %fusion.11 = (f32[32,16,128]{2,1,0:T(8,128)S(1)}, f32[32,16,128]{2,1,0:T(8,128)S(1)}) fusion(s32[128]{0:T(128)S(1)} %get-tuple-element.30, s32[128]{0:T(128)S(1)} %get-tuple-element.32, pred[128]{0:T(512)(128)(4,1)S(1)} %get-tuple-element.28, s32[]{:T(128)S(6)} %mul.40, s32[]{:T(128)S(6)} %select_n.32, s32[128]{0:T(128)S(1)} %get-tuple-element.31, ...), kind=kLoop, calls=%fused_computation.18 | loop fusion | flops 3014656 | bytes 526600 | tf_op jit(solution)/shard_map/sin | solution.py:563
  7.7 0.7 collective-permute-done.refs_3_
  8.4 1.8 %collective-permute-done.1.refs_4_ = bf16[272,128]{1,0:T(8,128)(2,1)S(1)} collective-permute-done((bf16[272,128]{1,0:T(8,128)(2,1)S(1)}, bf16[272,128]{1,0:T(8,128)(2,1)S(1)}, u32[]{:S(2)}, u32[]{:S(2)}) %collective-permute-start.1) | collective-permute-done | bytes 69664 | tf_op jit(solution)/shard_map/ppermute | solution.py:573
  10.2 0.5 collective-permute-done.2.refs_5_
  10.7 0.0 copy-done.5
  10.7 0.0 copy-done.8
  10.7 0.0 copy-start.4
  10.7 0.0 copy-start.6
  10.7 1.0 %shard_map.150 = (bf16[32,32,128]{2,1,0:T(8,128)(2,1)S(1)}, bf16[4,16,128]{2,1,0:T(8,128)(2,1)S(1)}) custom-call(bf16[256,512]{1,0:T(8,128)(2,1)S(1)} %copy-done.5, f32[256,8]{1,0:T(8,128)S(1)} %copy-done.8, bf16[272,128]{1,0:T(8,128)(2,1)S(1)} %get-tuple-element.14.refs_2_, bf16[272,128]{1,0:T(8,128)(2,1)S(1)} %collective-permute-done.refs_3_, ...), custom_call_target="tpu_custom_call" | custom-call | flops 134217728 | bytes 1351680 | tf_op jit(solution)/shard_map/pallas_call | solution.py:33
  11.8 0.0 copy-start
  11.8 0.0 copy-start.1
  11.8 15.1 %all_to_all.20.refs_0_ = bf16[32,32,128]{2,1,0:T(8,128)(2,1)S(1)} all-to-all(bf16[32,32,128]{2,1,0:T(8,128)(2,1)S(1)} %get-tuple-element.18), channel_id=1, replica_groups=mesh['rows'=8,'cols'=4] {'cols','rows'}, dimensions={0} | all-to-all | bytes 524288 | tf_op jit(solution)/shard_map/all_to_all | solution.py:567
  26.9 0.0 copy-done.4
  26.9 0.0 copy-done.6
  26.9 0.0 copy-done
  26.9 0.0 copy-done.1
  26.9 0.0 copy-start.11
  26.9 1.5 %shard_map.151 = bf16[32,32,256]{2,1,0:T(8,128)(2,1)S(1)} custom-call(bf16[32,32,128]{2,1,0:T(8,128)(2,1)S(1)} %all_to_all.20.refs_0_, f32[32,16,128]{2,1,0:T(8,128)S(1)} %get-tuple-element.27.refs_6_.refs_1_, f32[32,16,128]{2,1,0:T(8,128)S(1)} %get-tuple-element.26.refs_7_.refs_2_, bf16[512,256]{1,0:T(8,128)(2,1)S(1)} %copy-done.1, ...), custom_call_target="tpu_custom_call" | custom-call | flops 536870912 | bytes 2392064 | tf_op jit(solution)/shard_map/pallas_call | solution.py:33
  28.5 0.0 copy-start.2
  28.5 0.0 copy-start.7
  28.5 0.0 copy-start.10
  28.5 0.0 copy-start.12
  28.5 18.7 %all_to_all.21.refs_0_ = bf16[32,32,256]{2,1,0:T(8,128)(2,1)S(1)} all-to-all(bf16[32,32,256]{2,1,0:T(8,128)(2,1)S(1)} %shard_map.151), channel_id=1, replica_groups=mesh['rows'=8,'cols'=4] {'cols','rows'}, dimensions={0} | all-to-all | bytes 1048576 | tf_op jit(solution)/shard_map/all_to_all | solution.py:567
  47.2 0.0 copy-done.11
  47.2 0.0 copy-done.2
  47.2 0.0 copy-done.7
  47.2 0.0 copy-done.10
  47.2 0.0 copy-done.12
  47.2 3.7 %shard_map.152 = (bf16[32,32,256]{2,1,0:T(8,128)(2,1)S(1)}, bf16[4,16,128]{2,1,0:T(8,128)(2,1)S(1)}) custom-call(bf16[32,32,256]{2,1,0:T(8,128)(2,1)S(1)} %all_to_all.21.refs_0_, bf16[4,16,128]{2,1,0:T(8,128)(2,1)S(1)} %get-tuple-element.19.refs_1_, bf16[2,256,512]{2,1,0:T(8,128)(2,1)S(1)} %copy-done.2, f32[256,8]{1,0:T(8,128)S(1)} %copy-done.7, ...), custom_call_target="tpu_custom_call" | custom-call | flops 1610612736 | bytes 2473984 | tf_op jit(solution)/shard_map/pallas_call | solution.py:33
  51.0 0.0 copy-start.3
  51.0 18.4 %all_to_all.22.refs_0_ = bf16[32,32,256]{2,1,0:T(8,128)(2,1)S(1)} all-to-all(bf16[32,32,256]{2,1,0:T(8,128)(2,1)S(1)} %get-tuple-element.20), channel_id=1, replica_groups=mesh['rows'=8,'cols'=4] {'cols','rows'}, dimensions={0} | all-to-all | bytes 1048576 | tf_op jit(solution)/shard_map/all_to_all | solution.py:567
  69.4 0.0 copy-done.3
  69.4 1.7 %shard_map.153 = bf16[32,32,128]{2,1,0:T(8,128)(2,1)S(1)} custom-call(bf16[32,32,256]{2,1,0:T(8,128)(2,1)S(1)} %all_to_all.22.refs_0_, f32[32,16,128]{2,1,0:T(8,128)S(1)} %get-tuple-element.27.refs_6_.refs_1_, f32[32,16,128]{2,1,0:T(8,128)S(1)} %get-tuple-element.26.refs_7_.refs_2_, bf16[512,256]{1,0:T(8,128)(2,1)S(1)} %copy-done.1, ...), custom_call_target="tpu_custom_call" | custom-call | flops 536870912 | bytes 2392064 | tf_op jit(solution)/shard_map/pallas_call | solution.py:33
  71.1 12.4 %all_to_all.23.refs_0_ = bf16[32,32,128]{2,1,0:T(8,128)(2,1)S(1)} all-to-all(bf16[32,32,128]{2,1,0:T(8,128)(2,1)S(1)} %shard_map.153), channel_id=1, replica_groups=mesh['rows'=8,'cols'=4] {'cols','rows'}, dimensions={0} | all-to-all | bytes 524288 | tf_op jit(solution)/shard_map/all_to_all | solution.py:567
  83.5 1.3 %shard_map.154 = (bf16[272,128]{1,0:T(8,128)(2,1)S(1)}, bf16[272,128]{1,0:T(8,128)(2,1)S(1)}, bf16[272,128]{1,0:T(8,128)(2,1)S(1)}, bf16[272,128]{1,0:T(8,128)(2,1)S(1)}) custom-call(bf16[32,32,128]{2,1,0:T(8,128)(2,1)S(1)} %all_to_all.23.refs_0_, bf16[4,16,128]{2,1,0:T(8,128)(2,1)S(1)} %get-tuple-element.21.refs_1_, bf16[2,256,512]{2,1,0:T(8,128)(2,1)S(1)} %copy-done.2, ...), custom_call_target="tpu_custom_call" | custom-call | flops 134217728 | bytes 1089536 | tf_op jit(solution)/shard_map/pallas_call | solution.py:33
  84.8 0.9 collective-permute-start.3
  85.6 1.2 %collective-permute-start.4 = (bf16[272,128]{1,0:T(8,128)(2,1)S(1)}, bf16[272,128]{1,0:T(8,128)(2,1)S(1)}, u32[]{:S(2)}, u32[]{:S(2)}) collective-permute-start(bf16[272,128]{1,0:T(8,128)(2,1)S(1)} %get-tuple-element.24), channel_id=1, source_target_pairs={{0,1},{1,0},{2,3},{3,2},{4,5},{5,4},{6,7},{7,6},{8,9},{9,8},{10,11... | collective-permute-start | bytes 208904 | tf_op jit(solution)/shard_map/ppermute | solution.py:573
  86.8 1.5 %collective-permute-start.5 = (bf16[272,128]{1,0:T(8,128)(2,1)S(1)}, bf16[272,128]{1,0:T(8,128)(2,1)S(1)}, u32[]{:S(2)}, u32[]{:S(2)}) collective-permute-start(bf16[272,128]{1,0:T(8,128)(2,1)S(1)} %get-tuple-element.25), channel_id=1, source_target_pairs={{0,2},{1,3},{2,0},{3,1},{4,6},{5,7},{6,4},{7,5},{8,10},{9,11},{10,... | collective-permute-start | bytes 208904 | tf_op jit(solution)/shard_map/ppermute | solution.py:573
  88.4 2.4 %collective-permute-done.3.refs_1_ = bf16[272,128]{1,0:T(8,128)(2,1)S(1)} collective-permute-done((bf16[272,128]{1,0:T(8,128)(2,1)S(1)}, bf16[272,128]{1,0:T(8,128)(2,1)S(1)}, u32[]{:S(2)}, u32[]{:S(2)}) %collective-permute-start.3) | collective-permute-done | bytes 69664 | tf_op jit(solution)/shard_map/ppermute | solution.py:573
  90.8 0.3 collective-permute-done.4.refs_2_
  91.1 0.6 collective-permute-done.5.refs_3_
  91.7 1.0 %shard_map.155 = (f32[2,256,256]{2,1,0:T(8,128)}, f32[2,2,256]{2,1,0:T(2,128)}) custom-call(bf16[272,128]{1,0:T(8,128)(2,1)S(1)} %get-tuple-element.22.refs_0_, bf16[272,128]{1,0:T(8,128)(2,1)S(1)} %collective-permute-done.3.refs_1_, bf16[272,128]{1,0:T(8,128)(2,1)S(1)} %collective-permute-done.4.refs_2_, bf16[272,128]{1,0:T(8,128)(2,1)S(1)} %collective-permute-done.5.refs_3_), custom_call_target="tpu_custom_call" | custom-call | bytes 806912 | tf_op jit(solution)/shard_map/pallas_call | solution.py:33
  (3 shorter events, 0.0 us)
Async XLA Ops:
  0.6 1.1 %copy-start.9 = (f32[2,2,256]{2,1,0:T(2,128)S(1)}, f32[2,2,256]{2,1,0:T(2,128)}, u32[]{:S(2)}) copy-start(f32[2,2,256]{2,1,0:T(2,128)} %refs_1_.2) | copy-start | bytes 12292
  1.9 6.5 %collective-permute-start = (bf16[272,128]{1,0:T(8,128)(2,1)S(1)}, bf16[272,128]{1,0:T(8,128)(2,1)S(1)}, u32[]{:S(2)}, u32[]{:S(2)}) collective-permute-start(bf16[272,128]{1,0:T(8,128)(2,1)S(1)} %get-tuple-element.15), channel_id=1, source_target_pairs={{0,3},{1,2},{2,1},{3,0},{4,7},{5,6},{6,5},{7,4},{8,11},{9,10},{10,... | collective-permute-start | bytes 208904 | tf_op jit(solution)/shard_map/ppermute | solution.py:573
  5.9 4.3 %collective-permute-start.1 = (bf16[272,128]{1,0:T(8,128)(2,1)S(1)}, bf16[272,128]{1,0:T(8,128)(2,1)S(1)}, u32[]{:S(2)}, u32[]{:S(2)}) collective-permute-start(bf16[272,128]{1,0:T(8,128)(2,1)S(1)} %get-tuple-element.16), channel_id=1, source_target_pairs={{0,1},{1,0},{2,3},{3,2},{4,5},{5,4},{6,7},{7,6},{8,9},{9,8},{10,11... | collective-permute-start | bytes 208904 | tf_op jit(solution)/shard_map/ppermute | solution.py:573
  6.4 4.3 %collective-permute-start.2 = (bf16[272,128]{1,0:T(8,128)(2,1)S(1)}, bf16[272,128]{1,0:T(8,128)(2,1)S(1)}, u32[]{:S(2)}, u32[]{:S(2)}) collective-permute-start(bf16[272,128]{1,0:T(8,128)(2,1)S(1)} %get-tuple-element.17), channel_id=1, source_target_pairs={{0,2},{1,3},{2,0},{3,1},{4,6},{5,7},{6,4},{7,5},{8,10},{9,11},{10,... | collective-permute-start | bytes 208904 | tf_op jit(solution)/shard_map/ppermute | solution.py:573
  6.5 4.2 %copy-start.5 = (bf16[256,512]{1,0:T(8,128)(2,1)S(1)}, bf16[256,512]{1,0:T(8,128)(2,1)}, u32[]{:S(2)}) copy-start(bf16[256,512]{1,0:T(8,128)(2,1)} %constant.138.clone.refs_0_.refs_4_) | copy-start | bytes 786436
  6.6 4.2 %copy-start.8 = (f32[256,8]{1,0:T(8,128)S(1)}, f32[256,8]{1,0:T(8,128)}, u32[]{:S(2)}) copy-start(f32[256,8]{1,0:T(8,128)} %constant.139.clone.refs_1_.refs_5_) | copy-start | bytes 24580
  10.7 16.2 %copy-start.4 = (bf16[512,512]{1,0:T(8,128)(2,1)S(1)}, bf16[512,512]{1,0:T(8,128)(2,1)}, u32[]{:S(2)}) copy-start(bf16[512,512]{1,0:T(8,128)(2,1)} %constant.144.clone.refs_6_) | copy-start | bytes 1572868
  10.7 16.2 %copy-start.6 = (f32[2,32,128]{2,1,0:T(8,128)S(1)}, f32[2,32,128]{2,1,0:T(8,128)}, u32[]{:S(2)}) copy-start(f32[2,32,128]{2,1,0:T(8,128)} %constant.137.clone.refs_5_) | copy-start | bytes 98308
  11.8 15.1 %copy-start = (bf16[512,256]{1,0:T(8,128)(2,1)S(1)}, bf16[512,256]{1,0:T(8,128)(2,1)}, u32[]{:S(2)}) copy-start(bf16[512,256]{1,0:T(8,128)(2,1)} %constant.136.clone.refs_4_) | copy-start | bytes 786436
  11.8 15.1 %copy-start.1 = (bf16[512,256]{1,0:T(8,128)(2,1)S(1)}, bf16[512,256]{1,0:T(8,128)(2,1)}, u32[]{:S(2)}) copy-start(bf16[512,256]{1,0:T(8,128)(2,1)} %constant.135.clone.refs_3_) | copy-start | bytes 786436
  26.9 20.3 %copy-start.11 = (bf16[256,512]{1,0:T(8,128)(2,1)S(1)}, bf16[256,512]{1,0:T(8,128)(2,1)}, u32[]{:S(2)}) copy-start(bf16[256,512]{1,0:T(8,128)(2,1)} %constant.142.clone.refs_6_) | copy-start | bytes 786436
  28.5 18.7 %copy-start.2 = (bf16[2,256,512]{2,1,0:T(8,128)(2,1)S(1)}, bf16[2,256,512]{2,1,0:T(8,128)(2,1)}, u32[]{:S(2)}) copy-start(bf16[2,256,512]{2,1,0:T(8,128)(2,1)} %constant.140.clone.refs_2_) | copy-start | bytes 1572868
  28.5 18.7 %copy-start.7 = (f32[256,8]{1,0:T(8,128)S(1)}, f32[256,8]{1,0:T(8,128)}, u32[]{:S(2)}) copy-start(f32[256,8]{1,0:T(8,128)} %constant.141.clone.refs_3_) | copy-start | bytes 24580
  28.5 18.7 %copy-start.10 = (bf16[256,512]{1,0:T(8,128)(2,1)S(1)}, bf16[256,512]{1,0:T(8,128)(2,1)}, u32[]{:S(2)}) copy-start(bf16[256,512]{1,0:T(8,128)(2,1)} %constant.143.clone.refs_7_) | copy-start | bytes 786436
  28.5 18.7 %copy-start.12 = (f32[128,128]{1,0:T(8,128)S(1)}, f32[128,128]{1,0:T(8,128)}, u32[]{:S(2)}) copy-start(f32[128,128]{1,0:T(8,128)} %constant.146.clone.refs_8_) | copy-start | bytes 196612
  51.0 18.4 %copy-start.3 = (bf16[512,512]{1,0:T(8,128)(2,1)S(1)}, bf16[512,512]{1,0:T(8,128)(2,1)}, u32[]{:S(2)}) copy-start(bf16[512,512]{1,0:T(8,128)(2,1)} %constant.145.clone.refs_6_) | copy-start | bytes 1572868
  84.8 6.0 %collective-permute-start.3 = (bf16[272,128]{1,0:T(8,128)(2,1)S(1)}, bf16[272,128]{1,0:T(8,128)(2,1)S(1)}, u32[]{:S(2)}, u32[]{:S(2)}) collective-permute-start(bf16[272,128]{1,0:T(8,128)(2,1)S(1)} %get-tuple-element.23), channel_id=1, source_target_pairs={{0,3},{1,2},{2,1},{3,0},{4,7},{5,6},{6,5},{7,4},{8,11},{9,10},{10,... | collective-permute-start | bytes 208904 | tf_op jit(solution)/shard_map/ppermute | solution.py:573
  85.6 5.4 %collective-permute-start.4 = (bf16[272,128]{1,0:T(8,128)(2,1)S(1)}, bf16[272,128]{1,0:T(8,128)(2,1)S(1)}, u32[]{:S(2)}, u32[]{:S(2)}) collective-permute-start(bf16[272,128]{1,0:T(8,128)(2,1)S(1)} %get-tuple-element.24), channel_id=1, source_target_pairs={{0,1},{1,0},{2,3},{3,2},{4,5},{5,4},{6,7},{7,6},{8,9},{9,8},{10,11... | collective-permute-start | bytes 208904 | tf_op jit(solution)/shard_map/ppermute | solution.py:573
  86.8 4.9 %collective-permute-start.5 = (bf16[272,128]{1,0:T(8,128)(2,1)S(1)}, bf16[272,128]{1,0:T(8,128)(2,1)S(1)}, u32[]{:S(2)}, u32[]{:S(2)}) collective-permute-start(bf16[272,128]{1,0:T(8,128)(2,1)S(1)} %get-tuple-element.25), channel_id=1, source_target_pairs={{0,2},{1,3},{2,0},{3,1},{4,6},{5,7},{6,4},{7,5},{8,10},{9,11},{10,... | collective-permute-start | bytes 208904 | tf_op jit(solution)/shard_map/ppermute | solution.py:573
where the time goes:
time: 92.9 us; the launch traced here: 92.7 us
  blocking collectives  64.6 us (70%)
  Pallas kernels  10.4 us (11%)
  starting transfers between devices  8.19 us (9%)
  waiting for transfers between devices  6.37 us (7%)
  other arithmetic  2.21 us (2%)
    all_to_all x4, blocking collectives, exchange(): lax.all_to_all(chunks, ('cols', 'rows'), split_axis=0, concat_axis=0, til...  64.6 us
    pallas_call x7, Pallas kernels, call(): pl.pallas_call(body, out_shape=outs, scratch_shapes=list(scratch), compil...  10.4 us
    ppermute x6, starting transfers between devices, swap_columns(): lax.ppermute(chunk, 'cols', [(i, i ^ t) for i in range(count)])  8.19 us
    ppermute x6, waiting for transfers between devices, swap_columns(): lax.ppermute(chunk, 'cols', [(i, i ^ t) for i in range(count)])  6.37 us
  transfers between devices with their start and end apart: 6, of which 6 were waited for; matrix products, arithmetic and copies ran while one was open for 1% of the time, Pallas kernels for 0%

commit v1 on v0

--- a/solution.py
+++ b/solution.py
@@ -375,7 +375,7 @@
             cosine, sine = twist[0, k : k + 1, :], twist[1, k : k + 1, :]
             for offset, part in ((0, re * cosine - im * sine), (128, re * sine + im * cosine)):
                 rounded[k, :, offset : offset + 128] = part.astype(BF16)
-    group = D // 8 if sign > 0 else D
+    group = D // 4 if sign > 0 else D
     for start in range(0, D, group):
         place = slice(start, start + group)
 

time: 92.9 us -> 92.7 us (level)
  no operation moved by 1% of the time
where the time goes in v1:
time: 92.7 us; the launch traced here: 92.5 us
  blocking collectives  64.6 us (70%)
  Pallas kernels  10.2 us (11%)
  starting transfers between devices  8.19 us (9%)
  waiting for transfers between devices  6.37 us (7%)
  other arithmetic  2.21 us (2%)
    all_to_all x4, blocking collectives, exchange(): lax.all_to_all(chunks, ('cols', 'rows'), split_axis=0, concat_axis=0, til...  64.6 us
    pallas_call x7, Pallas kernels, call(): pl.pallas_call(body, out_shape=outs, scratch_shapes=list(scratch), compil...  10.2 us
    ppermute x6, starting transfers between devices, swap_columns(): lax.ppermute(chunk, 'cols', [(i, i ^ t) for i in range(count)])  8.19 us
    ppermute x6, waiting for transfers between devices, swap_columns(): lax.ppermute(chunk, 'cols', [(i, i ^ t) for i in range(count)])  6.37 us
  transfers between devices with their start and end apart: 6, of which 6 were waited for; matrix products, arithmetic and copies ran while one was open for 1% of the time, Pallas kernels for 0%

profile of v1, /device:TPU:0, one launch (start us, length us, event | category | flops | bytes accessed | tf_op | source)
XLA Modules:
  0.0 92.5 jit_solution(12213700293020509830)
XLA Ops:
  0.6 0.0 copy-start.9
  0.6 1.1 %convert_element_type.9.refs_0_ = bf16[2,256,256]{2,1,0:T(8,128)(2,1)S(1)} convert(f32[2,256,256]{2,1,0:T(8,128)} %param.14) | non-fusion elementwise | flops 131072 | bytes 786432 | tf_op jit(solution)/shard_map/convert_element_type | solution.py:612
  1.7 0.0 copy-done.9
  1.7 0.2 shard_map.149
  1.9 4.0 %collective-permute-start = (bf16[272,128]{1,0:T(8,128)(2,1)S(1)}, bf16[272,128]{1,0:T(8,128)(2,1)S(1)}, u32[]{:S(2)}, u32[]{:S(2)}) collective-permute-start(bf16[272,128]{1,0:T(8,128)(2,1)S(1)} %get-tuple-element.15), channel_id=1, source_target_pairs={{0,3},{1,2},{2,1},{3,0},{4,7},{5,6},{6,5},{7,4},{8,11},{9,10},{10,... | collective-permute-start | bytes 208904 | tf_op jit(solution)/shard_map/ppermute | solution.py:573
  5.9 0.5 collective-permute-start.1
  6.4 0.1 collective-permute-start.2
  6.5 0.0 copy-start.5
  6.6 0.0 copy-start.8
  6.6 1.1 %fusion.11 = (f32[32,16,128]{2,1,0:T(8,128)S(1)}, f32[32,16,128]{2,1,0:T(8,128)S(1)}) fusion(s32[128]{0:T(128)S(1)} %get-tuple-element.30, s32[128]{0:T(128)S(1)} %get-tuple-element.32, pred[128]{0:T(512)(128)(4,1)S(1)} %get-tuple-element.28, s32[]{:T(128)S(6)} %mul.40, s32[]{:T(128)S(6)} %select_n.32, s32[128]{0:T(128)S(1)} %get-tuple-element.31, ...), kind=kLoop, calls=%fused_computation.18 | loop fusion | flops 3014656 | bytes 526600 | tf_op jit(solution)/shard_map/sin | solution.py:563
  7.7 0.7 collective-permute-done.refs_3_
  8.4 1.8 %collective-permute-done.1.refs_4_ = bf16[272,128]{1,0:T(8,128)(2,1)S(1)} collective-permute-done((bf16[272,128]{1,0:T(8,128)(2,1)S(1)}, bf16[272,128]{1,0:T(8,128)(2,1)S(1)}, u32[]{:S(2)}, u32[]{:S(2)}) %collective-permute-start.1) | collective-permute-done | bytes 69664 | tf_op jit(solution)/shard_map/ppermute | solution.py:573
  10.2 0.5 collective-permute-done.2.refs_5_
  10.7 0.0 copy-done.5
  10.7 0.0 copy-done.8
  10.7 0.0 copy-start.4
  10.7 0.0 copy-start.6
  10.7 1.0 %shard_map.150 = (bf16[32,32,128]{2,1,0:T(8,128)(2,1)S(1)}, bf16[4,16,128]{2,1,0:T(8,128)(2,1)S(1)}) custom-call(bf16[256,512]{1,0:T(8,128)(2,1)S(1)} %copy-done.5, f32[256,8]{1,0:T(8,128)S(1)} %copy-done.8, bf16[272,128]{1,0:T(8,128)(2,1)S(1)} %get-tuple-element.14.refs_2_, bf16[272,128]{1,0:T(8,128)(2,1)S(1)} %collective-permute-done.refs_3_, ...), custom_call_target="tpu_custom_call" | custom-call | flops 134217728 | bytes 1351680 | tf_op jit(solution)/shard_map/pallas_call | solution.py:33
  11.8 0.0 copy-start
  11.8 0.0 copy-start.1
  11.8 15.1 %all_to_all.20.refs_0_ = bf16[32,32,128]{2,1,0:T(8,128)(2,1)S(1)} all-to-all(bf16[32,32,128]{2,1,0:T(8,128)(2,1)S(1)} %get-tuple-element.18), channel_id=1, replica_groups=mesh['rows'=8,'cols'=4] {'cols','rows'}, dimensions={0} | all-to-all | bytes 524288 | tf_op jit(solution)/shard_map/all_to_all | solution.py:567
  26.9 0.0 copy-done.4
  26.9 0.0 copy-done.6
  26.9 0.0 copy-done
  26.9 0.0 copy-done.1
  26.9 0.0 copy-start.11
  26.9 1.3 %shard_map.151 = bf16[32,32,256]{2,1,0:T(8,128)(2,1)S(1)} custom-call(bf16[32,32,128]{2,1,0:T(8,128)(2,1)S(1)} %all_to_all.20.refs_0_, f32[32,16,128]{2,1,0:T(8,128)S(1)} %get-tuple-element.27.refs_6_.refs_1_, f32[32,16,128]{2,1,0:T(8,128)S(1)} %get-tuple-element.26.refs_7_.refs_2_, bf16[512,256]{1,0:T(8,128)(2,1)S(1)} %copy-done.1, ...), custom_call_target="tpu_custom_call" | custom-call | flops 536870912 | bytes 2392064 | tf_op jit(solution)/shard_map/pallas_call | solution.py:33
  28.2 0.0 copy-start.2
  28.2 0.0 copy-start.7
  28.3 0.0 copy-start.10
  28.3 0.0 copy-start.12
  28.3 18.7 %all_to_all.21.refs_0_ = bf16[32,32,256]{2,1,0:T(8,128)(2,1)S(1)} all-to-all(bf16[32,32,256]{2,1,0:T(8,128)(2,1)S(1)} %shard_map.151), channel_id=1, replica_groups=mesh['rows'=8,'cols'=4] {'cols','rows'}, dimensions={0} | all-to-all | bytes 1048576 | tf_op jit(solution)/shard_map/all_to_all | solution.py:567
  47.0 0.0 copy-done.11
  47.0 0.0 copy-done.2
  47.0 0.0 copy-done.7
  47.0 0.0 copy-done.10
  47.0 0.0 copy-done.12
  47.0 3.7 %shard_map.152 = (bf16[32,32,256]{2,1,0:T(8,128)(2,1)S(1)}, bf16[4,16,128]{2,1,0:T(8,128)(2,1)S(1)}) custom-call(bf16[32,32,256]{2,1,0:T(8,128)(2,1)S(1)} %all_to_all.21.refs_0_, bf16[4,16,128]{2,1,0:T(8,128)(2,1)S(1)} %get-tuple-element.19.refs_1_, bf16[2,256,512]{2,1,0:T(8,128)(2,1)S(1)} %copy-done.2, f32[256,8]{1,0:T(8,128)S(1)} %copy-done.7, ...), custom_call_target="tpu_custom_call" | custom-call | flops 1610612736 | bytes 2473984 | tf_op jit(solution)/shard_map/pallas_call | solution.py:33
  50.8 0.0 copy-start.3
  50.8 18.4 %all_to_all.22.refs_0_ = bf16[32,32,256]{2,1,0:T(8,128)(2,1)S(1)} all-to-all(bf16[32,32,256]{2,1,0:T(8,128)(2,1)S(1)} %get-tuple-element.20), channel_id=1, replica_groups=mesh['rows'=8,'cols'=4] {'cols','rows'}, dimensions={0} | all-to-all | bytes 1048576 | tf_op jit(solution)/shard_map/all_to_all | solution.py:567
  69.2 0.0 copy-done.3
  69.2 1.7 %shard_map.153 = bf16[32,32,128]{2,1,0:T(8,128)(2,1)S(1)} custom-call(bf16[32,32,256]{2,1,0:T(8,128)(2,1)S(1)} %all_to_all.22.refs_0_, f32[32,16,128]{2,1,0:T(8,128)S(1)} %get-tuple-element.27.refs_6_.refs_1_, f32[32,16,128]{2,1,0:T(8,128)S(1)} %get-tuple-element.26.refs_7_.refs_2_, bf16[512,256]{1,0:T(8,128)(2,1)S(1)} %copy-done.1, ...), custom_call_target="tpu_custom_call" | custom-call | flops 536870912 | bytes 2392064 | tf_op jit(solution)/shard_map/pallas_call | solution.py:33
  70.9 12.4 %all_to_all.23.refs_0_ = bf16[32,32,128]{2,1,0:T(8,128)(2,1)S(1)} all-to-all(bf16[32,32,128]{2,1,0:T(8,128)(2,1)S(1)} %shard_map.153), channel_id=1, replica_groups=mesh['rows'=8,'cols'=4] {'cols','rows'}, dimensions={0} | all-to-all | bytes 524288 | tf_op jit(solution)/shard_map/all_to_all | solution.py:567
  83.3 1.3 %shard_map.154 = (bf16[272,128]{1,0:T(8,128)(2,1)S(1)}, bf16[272,128]{1,0:T(8,128)(2,1)S(1)}, bf16[272,128]{1,0:T(8,128)(2,1)S(1)}, bf16[272,128]{1,0:T(8,128)(2,1)S(1)}) custom-call(bf16[32,32,128]{2,1,0:T(8,128)(2,1)S(1)} %all_to_all.23.refs_0_, bf16[4,16,128]{2,1,0:T(8,128)(2,1)S(1)} %get-tuple-element.21.refs_1_, bf16[2,256,512]{2,1,0:T(8,128)(2,1)S(1)} %copy-done.2, ...), custom_call_target="tpu_custom_call" | custom-call | flops 134217728 | bytes 1089536 | tf_op jit(solution)/shard_map/pallas_call | solution.py:33
  84.6 0.9 collective-permute-start.3
  85.4 1.2 %collective-permute-start.4 = (bf16[272,128]{1,0:T(8,128)(2,1)S(1)}, bf16[272,128]{1,0:T(8,128)(2,1)S(1)}, u32[]{:S(2)}, u32[]{:S(2)}) collective-permute-start(bf16[272,128]{1,0:T(8,128)(2,1)S(1)} %get-tuple-element.24), channel_id=1, source_target_pairs={{0,1},{1,0},{2,3},{3,2},{4,5},{5,4},{6,7},{7,6},{8,9},{9,8},{10,11... | collective-permute-start | bytes 208904 | tf_op jit(solution)/shard_map/ppermute | solution.py:573
  86.6 1.5 %collective-permute-start.5 = (bf16[272,128]{1,0:T(8,128)(2,1)S(1)}, bf16[272,128]{1,0:T(8,128)(2,1)S(1)}, u32[]{:S(2)}, u32[]{:S(2)}) collective-permute-start(bf16[272,128]{1,0:T(8,128)(2,1)S(1)} %get-tuple-element.25), channel_id=1, source_target_pairs={{0,2},{1,3},{2,0},{3,1},{4,6},{5,7},{6,4},{7,5},{8,10},{9,11},{10,... | collective-permute-start | bytes 208904 | tf_op jit(solution)/shard_map/ppermute | solution.py:573
  88.1 2.4 %collective-permute-done.3.refs_1_ = bf16[272,128]{1,0:T(8,128)(2,1)S(1)} collective-permute-done((bf16[272,128]{1,0:T(8,128)(2,1)S(1)}, bf16[272,128]{1,0:T(8,128)(2,1)S(1)}, u32[]{:S(2)}, u32[]{:S(2)}) %collective-permute-start.3) | collective-permute-done | bytes 69664 | tf_op jit(solution)/shard_map/ppermute | solution.py:573
  90.6 0.3 collective-permute-done.4.refs_2_
  90.9 0.6 collective-permute-done.5.refs_3_
  91.5 1.0 %shard_map.155 = (f32[2,256,256]{2,1,0:T(8,128)}, f32[2,2,256]{2,1,0:T(2,128)}) custom-call(bf16[272,128]{1,0:T(8,128)(2,1)S(1)} %get-tuple-element.22.refs_0_, bf16[272,128]{1,0:T(8,128)(2,1)S(1)} %collective-permute-done.3.refs_1_, bf16[272,128]{1,0:T(8,128)(2,1)S(1)} %collective-permute-done.4.refs_2_, bf16[272,128]{1,0:T(8,128)(2,1)S(1)} %collective-permute-done.5.refs_3_), custom_call_target="tpu_custom_call" | custom-call | bytes 806912 | tf_op jit(solution)/shard_map/pallas_call | solution.py:33
  (3 shorter events, 0.0 us)
Async XLA Ops:
  0.6 1.1 %copy-start.9 = (f32[2,2,256]{2,1,0:T(2,128)S(1)}, f32[2,2,256]{2,1,0:T(2,128)}, u32[]{:S(2)}) copy-start(f32[2,2,256]{2,1,0:T(2,128)} %refs_1_.2) | copy-start | bytes 12292
  1.9 6.5 %collective-permute-start = (bf16[272,128]{1,0:T(8,128)(2,1)S(1)}, bf16[272,128]{1,0:T(8,128)(2,1)S(1)}, u32[]{:S(2)}, u32[]{:S(2)}) collective-permute-start(bf16[272,128]{1,0:T(8,128)(2,1)S(1)} %get-tuple-element.15), channel_id=1, source_target_pairs={{0,3},{1,2},{2,1},{3,0},{4,7},{5,6},{6,5},{7,4},{8,11},{9,10},{10,... | collective-permute-start | bytes 208904 | tf_op jit(solution)/shard_map/ppermute | solution.py:573
  5.9 4.3 %collective-permute-start.1 = (bf16[272,128]{1,0:T(8,128)(2,1)S(1)}, bf16[272,128]{1,0:T(8,128)(2,1)S(1)}, u32[]{:S(2)}, u32[]{:S(2)}) collective-permute-start(bf16[272,128]{1,0:T(8,128)(2,1)S(1)} %get-tuple-element.16), channel_id=1, source_target_pairs={{0,1},{1,0},{2,3},{3,2},{4,5},{5,4},{6,7},{7,6},{8,9},{9,8},{10,11... | collective-permute-start | bytes 208904 | tf_op jit(solution)/shard_map/ppermute | solution.py:573
  6.4 4.3 %collective-permute-start.2 = (bf16[272,128]{1,0:T(8,128)(2,1)S(1)}, bf16[272,128]{1,0:T(8,128)(2,1)S(1)}, u32[]{:S(2)}, u32[]{:S(2)}) collective-permute-start(bf16[272,128]{1,0:T(8,128)(2,1)S(1)} %get-tuple-element.17), channel_id=1, source_target_pairs={{0,2},{1,3},{2,0},{3,1},{4,6},{5,7},{6,4},{7,5},{8,10},{9,11},{10,... | collective-permute-start | bytes 208904 | tf_op jit(solution)/shard_map/ppermute | solution.py:573
  6.5 4.2 %copy-start.5 = (bf16[256,512]{1,0:T(8,128)(2,1)S(1)}, bf16[256,512]{1,0:T(8,128)(2,1)}, u32[]{:S(2)}) copy-start(bf16[256,512]{1,0:T(8,128)(2,1)} %constant.138.clone.refs_0_.refs_4_) | copy-start | bytes 786436
  6.6 4.2 %copy-start.8 = (f32[256,8]{1,0:T(8,128)S(1)}, f32[256,8]{1,0:T(8,128)}, u32[]{:S(2)}) copy-start(f32[256,8]{1,0:T(8,128)} %constant.139.clone.refs_1_.refs_5_) | copy-start | bytes 24580
  10.7 16.2 %copy-start.4 = (bf16[512,512]{1,0:T(8,128)(2,1)S(1)}, bf16[512,512]{1,0:T(8,128)(2,1)}, u32[]{:S(2)}) copy-start(bf16[512,512]{1,0:T(8,128)(2,1)} %constant.144.clone.refs_6_) | copy-start | bytes 1572868
  10.7 16.2 %copy-start.6 = (f32[2,32,128]{2,1,0:T(8,128)S(1)}, f32[2,32,128]{2,1,0:T(8,128)}, u32[]{:S(2)}) copy-start(f32[2,32,128]{2,1,0:T(8,128)} %constant.137.clone.refs_5_) | copy-start | bytes 98308
  11.8 15.1 %copy-start = (bf16[512,256]{1,0:T(8,128)(2,1)S(1)}, bf16[512,256]{1,0:T(8,128)(2,1)}, u32[]{:S(2)}) copy-start(bf16[512,256]{1,0:T(8,128)(2,1)} %constant.136.clone.refs_4_) | copy-start | bytes 786436
  11.8 15.1 %copy-start.1 = (bf16[512,256]{1,0:T(8,128)(2,1)S(1)}, bf16[512,256]{1,0:T(8,128)(2,1)}, u32[]{:S(2)}) copy-start(bf16[512,256]{1,0:T(8,128)(2,1)} %constant.135.clone.refs_3_) | copy-start | bytes 786436
  26.9 20.1 %copy-start.11 = (bf16[256,512]{1,0:T(8,128)(2,1)S(1)}, bf16[256,512]{1,0:T(8,128)(2,1)}, u32[]{:S(2)}) copy-start(bf16[256,512]{1,0:T(8,128)(2,1)} %constant.142.clone.refs_6_) | copy-start | bytes 786436
  28.2 18.7 %copy-start.2 = (bf16[2,256,512]{2,1,0:T(8,128)(2,1)S(1)}, bf16[2,256,512]{2,1,0:T(8,128)(2,1)}, u32[]{:S(2)}) copy-start(bf16[2,256,512]{2,1,0:T(8,128)(2,1)} %constant.140.clone.refs_2_) | copy-start | bytes 1572868
  28.2 18.7 %copy-start.7 = (f32[256,8]{1,0:T(8,128)S(1)}, f32[256,8]{1,0:T(8,128)}, u32[]{:S(2)}) copy-start(f32[256,8]{1,0:T(8,128)} %constant.141.clone.refs_3_) | copy-start | bytes 24580
  28.3 18.7 %copy-start.10 = (bf16[256,512]{1,0:T(8,128)(2,1)S(1)}, bf16[256,512]{1,0:T(8,128)(2,1)}, u32[]{:S(2)}) copy-start(bf16[256,512]{1,0:T(8,128)(2,1)} %constant.143.clone.refs_7_) | copy-start | bytes 786436
  28.3 18.7 %copy-start.12 = (f32[128,128]{1,0:T(8,128)S(1)}, f32[128,128]{1,0:T(8,128)}, u32[]{:S(2)}) copy-start(f32[128,128]{1,0:T(8,128)} %constant.146.clone.refs_8_) | copy-start | bytes 196612
  50.8 18.4 %copy-start.3 = (bf16[512,512]{1,0:T(8,128)(2,1)S(1)}, bf16[512,512]{1,0:T(8,128)(2,1)}, u32[]{:S(2)}) copy-start(bf16[512,512]{1,0:T(8,128)(2,1)} %constant.145.clone.refs_6_) | copy-start | bytes 1572868
  84.6 6.0 %collective-permute-start.3 = (bf16[272,128]{1,0:T(8,128)(2,1)S(1)}, bf16[272,128]{1,0:T(8,128)(2,1)S(1)}, u32[]{:S(2)}, u32[]{:S(2)}) collective-permute-start(bf16[272,128]{1,0:T(8,128)(2,1)S(1)} %get-tuple-element.23), channel_id=1, source_target_pairs={{0,3},{1,2},{2,1},{3,0},{4,7},{5,6},{6,5},{7,4},{8,11},{9,10},{10,... | collective-permute-start | bytes 208904 | tf_op jit(solution)/shard_map/ppermute | solution.py:573
  85.4 5.4 %collective-permute-start.4 = (bf16[272,128]{1,0:T(8,128)(2,1)S(1)}, bf16[272,128]{1,0:T(8,128)(2,1)S(1)}, u32[]{:S(2)}, u32[]{:S(2)}) collective-permute-start(bf16[272,128]{1,0:T(8,128)(2,1)S(1)} %get-tuple-element.24), channel_id=1, source_target_pairs={{0,1},{1,0},{2,3},{3,2},{4,5},{5,4},{6,7},{7,6},{8,9},{9,8},{10,11... | collective-permute-start | bytes 208904 | tf_op jit(solution)/shard_map/ppermute | solution.py:573
  86.6 4.9 %collective-permute-start.5 = (bf16[272,128]{1,0:T(8,128)(2,1)S(1)}, bf16[272,128]{1,0:T(8,128)(2,1)S(1)}, u32[]{:S(2)}, u32[]{:S(2)}) collective-permute-start(bf16[272,128]{1,0:T(8,128)(2,1)S(1)} %get-tuple-element.25), channel_id=1, source_target_pairs={{0,2},{1,3},{2,0},{3,1},{4,6},{5,7},{6,4},{7,5},{8,10},{9,11},{10,... | collective-permute-start | bytes 208904 | tf_op jit(solution)/shard_map/ppermute | solution.py:573

commit v2 on v1

--- a/solution.py
+++ b/solution.py
@@ -381,7 +381,7 @@
 
         def multiply(matrix):
             left = rounded[place].reshape(group * f, 256)
-            product = matmul(left, matrix[:256, :]) + matmul(left, matrix[256:, :])
+            product = matmul(left, matrix[:256, :])
             return product.reshape(group, f, 256)
 
         result = multiply(ahead)

time: 92.7 us -> 92.1 us (level)
  no operation moved by 1% of the time
where the time goes in v2:
time: 92.1 us; the launch traced here: 91.9 us
  blocking collectives  64.6 us (70%)
  Pallas kernels  9.64 us (10%)
  starting transfers between devices  8.19 us (9%)
  waiting for transfers between devices  6.37 us (7%)
  other arithmetic  2.21 us (2%)
    all_to_all x4, blocking collectives, exchange(): lax.all_to_all(chunks, ('cols', 'rows'), split_axis=0, concat_axis=0, til...  64.6 us
    pallas_call x7, Pallas kernels, call(): pl.pallas_call(body, out_shape=outs, scratch_shapes=list(scratch), compil...  9.64 us
    ppermute x6, starting transfers between devices, swap_columns(): lax.ppermute(chunk, 'cols', [(i, i ^ t) for i in range(count)])  8.19 us
    ppermute x6, waiting for transfers between devices, swap_columns(): lax.ppermute(chunk, 'cols', [(i, i ^ t) for i in range(count)])  6.37 us
  transfers between devices with their start and end apart: 6, of which 6 were waited for; matrix products, arithmetic and copies ran while one was open for 1% of the time, Pallas kernels for 0%

profile of v2, /device:TPU:0, one launch (start us, length us, event | category | flops | bytes accessed | tf_op | source)
XLA Modules:
  0.0 91.9 jit_solution(10917424479944237030)
XLA Ops:
  0.6 0.0 copy-start.9
  0.6 1.1 %convert_element_type.9.refs_0_ = bf16[2,256,256]{2,1,0:T(8,128)(2,1)S(1)} convert(f32[2,256,256]{2,1,0:T(8,128)} %param.14) | non-fusion elementwise | flops 131072 | bytes 786432 | tf_op jit(solution)/shard_map/convert_element_type | solution.py:612
  1.7 0.0 copy-done.9
  1.7 0.2 shard_map.149
  1.9 4.0 %collective-permute-start = (bf16[272,128]{1,0:T(8,128)(2,1)S(1)}, bf16[272,128]{1,0:T(8,128)(2,1)S(1)}, u32[]{:S(2)}, u32[]{:S(2)}) collective-permute-start(bf16[272,128]{1,0:T(8,128)(2,1)S(1)} %get-tuple-element.15), channel_id=1, source_target_pairs={{0,3},{1,2},{2,1},{3,0},{4,7},{5,6},{6,5},{7,4},{8,11},{9,10},{10,... | collective-permute-start | bytes 208904 | tf_op jit(solution)/shard_map/ppermute | solution.py:573
  5.9 0.5 collective-permute-start.1
  6.4 0.1 collective-permute-start.2
  6.5 0.0 copy-start.5
  6.6 0.0 copy-start.8
  6.6 1.1 %fusion.11 = (f32[32,16,128]{2,1,0:T(8,128)S(1)}, f32[32,16,128]{2,1,0:T(8,128)S(1)}) fusion(s32[128]{0:T(128)S(1)} %get-tuple-element.30, s32[128]{0:T(128)S(1)} %get-tuple-element.32, pred[128]{0:T(512)(128)(4,1)S(1)} %get-tuple-element.28, s32[]{:T(128)S(6)} %mul.40, s32[]{:T(128)S(6)} %select_n.32, s32[128]{0:T(128)S(1)} %get-tuple-element.31, ...), kind=kLoop, calls=%fused_computation.18 | loop fusion | flops 3014656 | bytes 526600 | tf_op jit(solution)/shard_map/sin | solution.py:563
  7.7 0.7 collective-permute-done.refs_3_
  8.4 1.8 %collective-permute-done.1.refs_4_ = bf16[272,128]{1,0:T(8,128)(2,1)S(1)} collective-permute-done((bf16[272,128]{1,0:T(8,128)(2,1)S(1)}, bf16[272,128]{1,0:T(8,128)(2,1)S(1)}, u32[]{:S(2)}, u32[]{:S(2)}) %collective-permute-start.1) | collective-permute-done | bytes 69664 | tf_op jit(solution)/shard_map/ppermute | solution.py:573
  10.2 0.5 collective-permute-done.2.refs_5_
  10.7 0.0 copy-done.5
  10.7 0.0 copy-done.8
  10.7 0.0 copy-start.4
  10.7 0.0 copy-start.6
  10.7 1.0 %shard_map.150 = (bf16[32,32,128]{2,1,0:T(8,128)(2,1)S(1)}, bf16[4,16,128]{2,1,0:T(8,128)(2,1)S(1)}) custom-call(bf16[256,512]{1,0:T(8,128)(2,1)S(1)} %copy-done.5, f32[256,8]{1,0:T(8,128)S(1)} %copy-done.8, bf16[272,128]{1,0:T(8,128)(2,1)S(1)} %get-tuple-element.14.refs_2_, bf16[272,128]{1,0:T(8,128)(2,1)S(1)} %collective-permute-done.refs_3_, ...), custom_call_target="tpu_custom_call" | custom-call | flops 134217728 | bytes 1351680 | tf_op jit(solution)/shard_map/pallas_call | solution.py:33
  11.8 0.0 copy-start
  11.8 0.0 copy-start.1
  11.8 15.1 %all_to_all.20.refs_0_ = bf16[32,32,128]{2,1,0:T(8,128)(2,1)S(1)} all-to-all(bf16[32,32,128]{2,1,0:T(8,128)(2,1)S(1)} %get-tuple-element.18), channel_id=1, replica_groups=mesh['rows'=8,'cols'=4] {'cols','rows'}, dimensions={0} | all-to-all | bytes 524288 | tf_op jit(solution)/shard_map/all_to_all | solution.py:567
  26.9 0.0 copy-done.4
  26.9 0.0 copy-done.6
  26.9 0.0 copy-done
  26.9 0.0 copy-done.1
  26.9 0.0 copy-start.11
  26.9 1.2 %shard_map.151 = bf16[32,32,256]{2,1,0:T(8,128)(2,1)S(1)} custom-call(bf16[32,32,128]{2,1,0:T(8,128)(2,1)S(1)} %all_to_all.20.refs_0_, f32[32,16,128]{2,1,0:T(8,128)S(1)} %get-tuple-element.27.refs_6_.refs_1_, f32[32,16,128]{2,1,0:T(8,128)S(1)} %get-tuple-element.26.refs_7_.refs_2_, bf16[512,256]{1,0:T(8,128)(2,1)S(1)} %copy-done.1, ...), custom_call_target="tpu_custom_call" | custom-call | flops 536870912 | bytes 2392064 | tf_op jit(solution)/shard_map/pallas_call | solution.py:33
  28.1 0.0 copy-start.2
  28.1 0.0 copy-start.7
  28.1 0.0 copy-start.10
  28.1 0.0 copy-start.12
  28.1 18.7 %all_to_all.21.refs_0_ = bf16[32,32,256]{2,1,0:T(8,128)(2,1)S(1)} all-to-all(bf16[32,32,256]{2,1,0:T(8,128)(2,1)S(1)} %shard_map.151), channel_id=1, replica_groups=mesh['rows'=8,'cols'=4] {'cols','rows'}, dimensions={0} | all-to-all | bytes 1048576 | tf_op jit(solution)/shard_map/all_to_all | solution.py:567
  46.8 0.0 copy-done.11
  46.8 0.0 copy-done.2
  46.8 0.0 copy-done.7
  46.8 0.0 copy-done.10
  46.8 0.0 copy-done.12
  46.8 3.7 %shard_map.152 = (bf16[32,32,256]{2,1,0:T(8,128)(2,1)S(1)}, bf16[4,16,128]{2,1,0:T(8,128)(2,1)S(1)}) custom-call(bf16[32,32,256]{2,1,0:T(8,128)(2,1)S(1)} %all_to_all.21.refs_0_, bf16[4,16,128]{2,1,0:T(8,128)(2,1)S(1)} %get-tuple-element.19.refs_1_, bf16[2,256,512]{2,1,0:T(8,128)(2,1)S(1)} %copy-done.2, f32[256,8]{1,0:T(8,128)S(1)} %copy-done.7, ...), custom_call_target="tpu_custom_call" | custom-call | flops 1610612736 | bytes 2473984 | tf_op jit(solution)/shard_map/pallas_call | solution.py:33
  50.6 0.0 copy-start.3
  50.6 18.4 %all_to_all.22.refs_0_ = bf16[32,32,256]{2,1,0:T(8,128)(2,1)S(1)} all-to-all(bf16[32,32,256]{2,1,0:T(8,128)(2,1)S(1)} %get-tuple-element.20), channel_id=1, replica_groups=mesh['rows'=8,'cols'=4] {'cols','rows'}, dimensions={0} | all-to-all | bytes 1048576 | tf_op jit(solution)/shard_map/all_to_all | solution.py:567
  69.0 0.0 copy-done.3
  69.0 1.3 %shard_map.153 = bf16[32,32,128]{2,1,0:T(8,128)(2,1)S(1)} custom-call(bf16[32,32,256]{2,1,0:T(8,128)(2,1)S(1)} %all_to_all.22.refs_0_, f32[32,16,128]{2,1,0:T(8,128)S(1)} %get-tuple-element.27.refs_6_.refs_1_, f32[32,16,128]{2,1,0:T(8,128)S(1)} %get-tuple-element.26.refs_7_.refs_2_, bf16[512,256]{1,0:T(8,128)(2,1)S(1)} %copy-done.1, ...), custom_call_target="tpu_custom_call" | custom-call | flops 536870912 | bytes 2392064 | tf_op jit(solution)/shard_map/pallas_call | solution.py:33
  70.3 12.4 %all_to_all.23.refs_0_ = bf16[32,32,128]{2,1,0:T(8,128)(2,1)S(1)} all-to-all(bf16[32,32,128]{2,1,0:T(8,128)(2,1)S(1)} %shard_map.153), channel_id=1, replica_groups=mesh['rows'=8,'cols'=4] {'cols','rows'}, dimensions={0} | all-to-all | bytes 524288 | tf_op jit(solution)/shard_map/all_to_all | solution.py:567
  82.7 1.3 %shard_map.154 = (bf16[272,128]{1,0:T(8,128)(2,1)S(1)}, bf16[272,128]{1,0:T(8,128)(2,1)S(1)}, bf16[272,128]{1,0:T(8,128)(2,1)S(1)}, bf16[272,128]{1,0:T(8,128)(2,1)S(1)}) custom-call(bf16[32,32,128]{2,1,0:T(8,128)(2,1)S(1)} %all_to_all.23.refs_0_, bf16[4,16,128]{2,1,0:T(8,128)(2,1)S(1)} %get-tuple-element.21.refs_1_, bf16[2,256,512]{2,1,0:T(8,128)(2,1)S(1)} %copy-done.2, ...), custom_call_target="tpu_custom_call" | custom-call | flops 134217728 | bytes 1089536 | tf_op jit(solution)/shard_map/pallas_call | solution.py:33
  84.0 0.9 collective-permute-start.3
  84.9 1.2 %collective-permute-start.4 = (bf16[272,128]{1,0:T(8,128)(2,1)S(1)}, bf16[272,128]{1,0:T(8,128)(2,1)S(1)}, u32[]{:S(2)}, u32[]{:S(2)}) collective-permute-start(bf16[272,128]{1,0:T(8,128)(2,1)S(1)} %get-tuple-element.24), channel_id=1, source_target_pairs={{0,1},{1,0},{2,3},{3,2},{4,5},{5,4},{6,7},{7,6},{8,9},{9,8},{10,11... | collective-permute-start | bytes 208904 | tf_op jit(solution)/shard_map/ppermute | solution.py:573
  86.1 1.5 %collective-permute-start.5 = (bf16[272,128]{1,0:T(8,128)(2,1)S(1)}, bf16[272,128]{1,0:T(8,128)(2,1)S(1)}, u32[]{:S(2)}, u32[]{:S(2)}) collective-permute-start(bf16[272,128]{1,0:T(8,128)(2,1)S(1)} %get-tuple-element.25), channel_id=1, source_target_pairs={{0,2},{1,3},{2,0},{3,1},{4,6},{5,7},{6,4},{7,5},{8,10},{9,11},{10,... | collective-permute-start | bytes 208904 | tf_op jit(solution)/shard_map/ppermute | solution.py:573
  87.6 2.4 %collective-permute-done.3.refs_1_ = bf16[272,128]{1,0:T(8,128)(2,1)S(1)} collective-permute-done((bf16[272,128]{1,0:T(8,128)(2,1)S(1)}, bf16[272,128]{1,0:T(8,128)(2,1)S(1)}, u32[]{:S(2)}, u32[]{:S(2)}) %collective-permute-start.3) | collective-permute-done | bytes 69664 | tf_op jit(solution)/shard_map/ppermute | solution.py:573
  90.0 0.3 collective-permute-done.4.refs_2_
  90.3 0.6 collective-permute-done.5.refs_3_
  90.9 1.0 %shard_map.155 = (f32[2,256,256]{2,1,0:T(8,128)}, f32[2,2,256]{2,1,0:T(2,128)}) custom-call(bf16[272,128]{1,0:T(8,128)(2,1)S(1)} %get-tuple-element.22.refs_0_, bf16[272,128]{1,0:T(8,128)(2,1)S(1)} %collective-permute-done.3.refs_1_, bf16[272,128]{1,0:T(8,128)(2,1)S(1)} %collective-permute-done.4.refs_2_, bf16[272,128]{1,0:T(8,128)(2,1)S(1)} %collective-permute-done.5.refs_3_), custom_call_target="tpu_custom_call" | custom-call | bytes 806912 | tf_op jit(solution)/shard_map/pallas_call | solution.py:33
  (3 shorter events, 0.0 us)
Async XLA Ops:
  0.6 1.1 %copy-start.9 = (f32[2,2,256]{2,1,0:T(2,128)S(1)}, f32[2,2,256]{2,1,0:T(2,128)}, u32[]{:S(2)}) copy-start(f32[2,2,256]{2,1,0:T(2,128)} %refs_1_.2) | copy-start | bytes 12292
  1.9 6.5 %collective-permute-start = (bf16[272,128]{1,0:T(8,128)(2,1)S(1)}, bf16[272,128]{1,0:T(8,128)(2,1)S(1)}, u32[]{:S(2)}, u32[]{:S(2)}) collective-permute-start(bf16[272,128]{1,0:T(8,128)(2,1)S(1)} %get-tuple-element.15), channel_id=1, source_target_pairs={{0,3},{1,2},{2,1},{3,0},{4,7},{5,6},{6,5},{7,4},{8,11},{9,10},{10,... | collective-permute-start | bytes 208904 | tf_op jit(solution)/shard_map/ppermute | solution.py:573
  5.9 4.3 %collective-permute-start.1 = (bf16[272,128]{1,0:T(8,128)(2,1)S(1)}, bf16[272,128]{1,0:T(8,128)(2,1)S(1)}, u32[]{:S(2)}, u32[]{:S(2)}) collective-permute-start(bf16[272,128]{1,0:T(8,128)(2,1)S(1)} %get-tuple-element.16), channel_id=1, source_target_pairs={{0,1},{1,0},{2,3},{3,2},{4,5},{5,4},{6,7},{7,6},{8,9},{9,8},{10,11... | collective-permute-start | bytes 208904 | tf_op jit(solution)/shard_map/ppermute | solution.py:573
  6.4 4.3 %collective-permute-start.2 = (bf16[272,128]{1,0:T(8,128)(2,1)S(1)}, bf16[272,128]{1,0:T(8,128)(2,1)S(1)}, u32[]{:S(2)}, u32[]{:S(2)}) collective-permute-start(bf16[272,128]{1,0:T(8,128)(2,1)S(1)} %get-tuple-element.17), channel_id=1, source_target_pairs={{0,2},{1,3},{2,0},{3,1},{4,6},{5,7},{6,4},{7,5},{8,10},{9,11},{10,... | collective-permute-start | bytes 208904 | tf_op jit(solution)/shard_map/ppermute | solution.py:573
  6.5 4.2 %copy-start.5 = (bf16[256,512]{1,0:T(8,128)(2,1)S(1)}, bf16[256,512]{1,0:T(8,128)(2,1)}, u32[]{:S(2)}) copy-start(bf16[256,512]{1,0:T(8,128)(2,1)} %constant.138.clone.refs_0_.refs_4_) | copy-start | bytes 786436
  6.6 4.2 %copy-start.8 = (f32[256,8]{1,0:T(8,128)S(1)}, f32[256,8]{1,0:T(8,128)}, u32[]{:S(2)}) copy-start(f32[256,8]{1,0:T(8,128)} %constant.139.clone.refs_1_.refs_5_) | copy-start | bytes 24580
  10.7 16.2 %copy-start.4 = (bf16[512,512]{1,0:T(8,128)(2,1)S(1)}, bf16[512,512]{1,0:T(8,128)(2,1)}, u32[]{:S(2)}) copy-start(bf16[512,512]{1,0:T(8,128)(2,1)} %constant.144.clone.refs_6_) | copy-start | bytes 1572868
  10.7 16.2 %copy-start.6 = (f32[2,32,128]{2,1,0:T(8,128)S(1)}, f32[2,32,128]{2,1,0:T(8,128)}, u32[]{:S(2)}) copy-start(f32[2,32,128]{2,1,0:T(8,128)} %constant.137.clone.refs_5_) | copy-start | bytes 98308
  11.8 15.1 %copy-start = (bf16[512,256]{1,0:T(8,128)(2,1)S(1)}, bf16[512,256]{1,0:T(8,128)(2,1)}, u32[]{:S(2)}) copy-start(bf16[512,256]{1,0:T(8,128)(2,1)} %constant.136.clone.refs_4_) | copy-start | bytes 786436
  11.8 15.1 %copy-start.1 = (bf16[512,256]{1,0:T(8,128)(2,1)S(1)}, bf16[512,256]{1,0:T(8,128)(2,1)}, u32[]{:S(2)}) copy-start(bf16[512,256]{1,0:T(8,128)(2,1)} %constant.135.clone.refs_3_) | copy-start | bytes 786436
  26.9 19.9 %copy-start.11 = (bf16[256,512]{1,0:T(8,128)(2,1)S(1)}, bf16[256,512]{1,0:T(8,128)(2,1)}, u32[]{:S(2)}) copy-start(bf16[256,512]{1,0:T(8,128)(2,1)} %constant.142.clone.refs_6_) | copy-start | bytes 786436
  28.1 18.7 %copy-start.2 = (bf16[2,256,512]{2,1,0:T(8,128)(2,1)S(1)}, bf16[2,256,512]{2,1,0:T(8,128)(2,1)}, u32[]{:S(2)}) copy-start(bf16[2,256,512]{2,1,0:T(8,128)(2,1)} %constant.140.clone.refs_2_) | copy-start | bytes 1572868
  28.1 18.7 %copy-start.7 = (f32[256,8]{1,0:T(8,128)S(1)}, f32[256,8]{1,0:T(8,128)}, u32[]{:S(2)}) copy-start(f32[256,8]{1,0:T(8,128)} %constant.141.clone.refs_3_) | copy-start | bytes 24580
  28.1 18.7 %copy-start.10 = (bf16[256,512]{1,0:T(8,128)(2,1)S(1)}, bf16[256,512]{1,0:T(8,128)(2,1)}, u32[]{:S(2)}) copy-start(bf16[256,512]{1,0:T(8,128)(2,1)} %constant.143.clone.refs_7_) | copy-start | bytes 786436
  28.1 18.7 %copy-start.12 = (f32[128,128]{1,0:T(8,128)S(1)}, f32[128,128]{1,0:T(8,128)}, u32[]{:S(2)}) copy-start(f32[128,128]{1,0:T(8,128)} %constant.146.clone.refs_8_) | copy-start | bytes 196612
  50.6 18.4 %copy-start.3 = (bf16[512,512]{1,0:T(8,128)(2,1)S(1)}, bf16[512,512]{1,0:T(8,128)(2,1)}, u32[]{:S(2)}) copy-start(bf16[512,512]{1,0:T(8,128)(2,1)} %constant.145.clone.refs_6_) | copy-start | bytes 1572868
  84.0 6.0 %collective-permute-start.3 = (bf16[272,128]{1,0:T(8,128)(2,1)S(1)}, bf16[272,128]{1,0:T(8,128)(2,1)S(1)}, u32[]{:S(2)}, u32[]{:S(2)}) collective-permute-start(bf16[272,128]{1,0:T(8,128)(2,1)S(1)} %get-tuple-element.23), channel_id=1, source_target_pairs={{0,3},{1,2},{2,1},{3,0},{4,7},{5,6},{6,5},{7,4},{8,11},{9,10},{10,... | collective-permute-start | bytes 208904 | tf_op jit(solution)/shard_map/ppermute | solution.py:573
  84.9 5.4 %collective-permute-start.4 = (bf16[272,128]{1,0:T(8,128)(2,1)S(1)}, bf16[272,128]{1,0:T(8,128)(2,1)S(1)}, u32[]{:S(2)}, u32[]{:S(2)}) collective-permute-start(bf16[272,128]{1,0:T(8,128)(2,1)S(1)} %get-tuple-element.24), channel_id=1, source_target_pairs={{0,1},{1,0},{2,3},{3,2},{4,5},{5,4},{6,7},{7,6},{8,9},{9,8},{10,11... | collective-permute-start | bytes 208904 | tf_op jit(solution)/shard_map/ppermute | solution.py:573
  86.1 4.9 %collective-permute-start.5 = (bf16[272,128]{1,0:T(8,128)(2,1)S(1)}, bf16[272,128]{1,0:T(8,128)(2,1)S(1)}, u32[]{:S(2)}, u32[]{:S(2)}) collective-permute-start(bf16[272,128]{1,0:T(8,128)(2,1)S(1)} %get-tuple-element.25), channel_id=1, source_target_pairs={{0,2},{1,3},{2,0},{3,1},{4,6},{5,7},{6,4},{7,5},{8,10},{9,11},{10,... | collective-permute-start | bytes 208904 | tf_op jit(solution)/shard_map/ppermute | solution.py:573
